TPU v7x, 32 devices: a whole 2x2x4 slice. The times are simulated.
32 devices in a mesh: chain: 16 (over z, y, x), block: 2 (over core).
Axes of the slice: x: 2, y: 2, z: 4, core: 2. Of those that a mesh axis runs over, the one named last changes fastest.
Arguments:
- site_tensors: bfloat16 [16, 32, 2, 256, 256], P('chain', 'block'), may hold values from -4.5 to 7.5
- sketch: bfloat16 [512, 256], replicated, may hold values from -6 to 6
- bond_sizes: int32 [16, 2, 32], P('chain'), may hold values from 32 to 256, as said below
- kept_ranks: int32 [16, 2, 32], P('chain'), may hold values from 0 to 256, as said below
- couplings: float32 [16, 2, 3], P('chain'), may hold values from -1 to 2.5, as said below
Outputs:
- updated_sites: bfloat16 [16, 32, 2, 256, 256], P('chain', 'block')
Inputs may be any that keep to these rules, and one draw needn't show every extreme that they name: bond_sizes[i, 1] are the block sizes of the bond right of site i and bond_sizes[i, 0] equals bond_sizes[i - 1 mod 16, 1]; every bond has a block of exactly 256. kept_ranks[i, 1] belongs to the bond right of site i and kept_ranks[i, 0] equals kept_ranks[i - 1 mod 16, 1]; a count never exceeds that block's size; some block keeps exactly 256. couplings[i, 0] equals couplings[i - 1 mod 16, 1]; hopping lies in 0.5 to 2.5, the other two in -1 to 1.
All inputs are finite; a program needn't handle non-finite values.
Results may differ from a plain program's by a relative error of at most 0.035.
Values may be sent and summed in bfloat16 or wider, within the bound.
No kernel may reach another device: no remote copies, remote signals or barrier semaphores. Data moves between devices by JAX's collectives and lax.ppermute only.
A program may use at most 128 MiB of HBM per device.

v0:
```python
import math

import jax
import jax.numpy as jnp
from jax import lax
from jax.experimental import pallas as pl
from jax.experimental.pallas import tpu as pltpu
from jax.sharding import PartitionSpec as P

tau_step = 0.5
SUB = 8
LANES = 128
PANEL = 32
PART = 8
UNROLL = 2
FIRST = (((0,), (0,)), ((), ()))
LAST = (((1,), (1,)), ((), ()))
PLAIN = (((1,), (0,)), ((), ()))


def gate_terms(hopping, ising_term, field_term):
    rotation = 0.5 * tau_step * hopping
    middle_scale = jnp.exp(0.25 * tau_step * ising_term)
    weight_empty = jnp.exp(-tau_step * (0.25 * ising_term - 0.5 * field_term))
    weight_full = jnp.exp(-tau_step * (0.25 * ising_term + 0.5 * field_term))
    grown, shrunk = jnp.exp(rotation), jnp.exp(-rotation)
    weight_stay = middle_scale * (0.5 * (grown + shrunk))
    weight_swap = -middle_scale * (0.5 * (grown - shrunk))
    return weight_empty, weight_stay, weight_swap, weight_full


def dot(left, right, dims):
    return lax.dot_general(left, right, dims, preferred_element_type=jnp.float32)


def spread(row, lane_index):
    return jnp.take_along_axis(row, lane_index, axis=1)


def refined_reciprocal(value):
    guess = pltpu.reciprocal(value, approx=True)
    return guess * (2.0 - value * guess)


def factor_panel(rows_ref, first, tile):
    lanes = rows_ref.shape[0] * LANES
    lane = lax.broadcasted_iota(jnp.int32, (SUB, lanes), 1)
    zero = jnp.zeros((SUB, LANES), jnp.int32)
    mine = slice(tile * LANES, (tile + 1) * LANES)
    stop = first + PANEL

    def load(index):
        at = slice(index * SUB, (index + 1) * SUB)
        return jnp.concatenate([rows_ref[half, at, :] for half in range(lanes // LANES)], axis=1)

    def wide(value):
        return jnp.concatenate([value] * (lanes // LANES), axis=1)

    def store(index, value):
        at = slice(index * SUB, (index + 1) * SUB)
        for half in range(lanes // LANES):
            rows_ref[half, at, :] = value[:, half * LANES : (half + 1) * LANES]

    for start in range(0, PANEL, PART):
        rows = [load(start + i) for i in range(PART)]
        base = first - tile * LANES + start
        entry = [
            [spread(rows[i][:, mine], base + j + zero) if j >= i else None for j in range(PART)]
            for i in range(PART)
        ]
        later = []
        for step in range(PART):
            k = first + start + step
            inverted = refined_reciprocal(entry[step][step])
            unit = jnp.where(lane == k, 1.0, rows[step])
            for other in range(step + 1, PART):
                ratio = entry[step][other] * inverted
                for column in range(other, PART):
                    entry[other][column] = entry[other][column] - ratio * entry[step][column]
                rows[other] = jnp.where(lane == k, 0.0, rows[other]) - wide(ratio) * unit
            done = jnp.where((lane > k) & (lane < stop), 0.0, unit)
            store(start + step, done * wide(lax.rsqrt(entry[step][step])))
            hidden = jnp.where((lane > k) & (lane < first + start + PART), 0.0, unit)
            later.append(hidden * wide(inverted))
        for i in range(start + PART, PANEL):
            hide = (lane >= first + start) & (lane < first + start + PART)
            row = jnp.where(hide, 0.0, load(i))
            for step in range(PART):
                row = row - wide(spread(rows[step][:, mine], first - tile * LANES + i + zero)) * later[step]
            store(i, row)


def in_parts(value):
    high = value.astype(jnp.bfloat16)
    rest = value - high.astype(jnp.float32)
    middle = rest.astype(jnp.bfloat16)
    return high, middle, (rest - middle.astype(jnp.float32)).astype(jnp.bfloat16)


def run_copies(plan, semaphores):
    copies = [
        pltpu.make_async_copy(source, place, semaphores.at[index])
        for index, (source, place) in enumerate(plan)
    ]
    for copy in copies:
        copy.start()
    for copy in copies:
        copy.wait()


def run_by_parity(even_plan, odd_plan, semaphores):
    is_even = lax.rem(lax.axis_index("chain"), 2) == 0

    @pl.when(is_even)
    def _():
        run_copies(even_plan, semaphores)

    @pl.when(jnp.logical_not(is_even))
    def _():
        run_copies(odd_plan, semaphores)


def chunk_sizes(half):
    early = max(half // 2, 1)
    return early, early - 1


def cut(line, first, count, place):
    plan = []
    for source, start, size in line:
        low, high = max(first, start), min(first + count, start + size)
        if low < high:
            plan.append((source(low - start, high - low), place(low - first, high - low)))
    return plan


def whole(ref):
    return lambda start, size: ref.at[pl.ds(start, size)]


def plane(ref, s):
    return lambda start, size: ref.at[pl.ds(start, size), s]


def first_plans(first_of, count, half, early, operands, left, right):
    own, got_early, got_late, edge, corner = operands
    late, sectors = half - early, 2 * half
    if first_of[0] == 0:
        even_own, odd_own = (own, 0, early + 1), (own, sectors - early - 1, early + 1)
    else:
        even_own, odd_own = (own, early - 1, late + 2), (own, half - 1, late + 2)

    def plans(first, left_line, right_line, extra):
        zero_line = [(plane(ref, 0), start, size) for ref, start, size in right_line]
        one_line = [(plane(ref, 1), start, size) for ref, start, size in right_line]
        return [
            *cut([(whole(ref), start, size) for ref, start, size in left_line], first - 1, count + 1, whole(left)),
            *cut(zero_line, first, count + 1, plane(right, 0)),
            *cut(one_line + extra, first - 1, count + 1, plane(right, 1)),
        ]

    even = plans(
        first_of[0],
        [(edge, -1, 1), even_own],
        [(got_early, 0, early + 1), (got_late, early + 1, late)],
        [(whole(corner), -1, 1)],
    )
    odd = plans(
        first_of[1],
        [(got_late, half - 1, late), (got_early, sectors - early - 1, early + 1)],
        [odd_own, (edge, sectors, 1)],
        [],
    )
    return even, odd


def second_plans(first_of, count, half, early, operands, left, right):
    keep_early, keep_late, carried_early, carried_late, far, near = operands
    late, sectors = half - early, 2 * half

    def plans(first, left_line, right_line):
        return [
            *cut([(whole(ref), start, size) for ref, start, size in left_line], first - 1, count + 1, whole(left)),
            *cut([(whole(ref), start, size) for ref, start, size in right_line], first, count + 1, whole(right)),
        ]

    even = plans(
        first_of[0],
        [(far, -1, 1), (carried_early, 0, early), (carried_late, early, late)],
        [(keep_early, 0, early), (keep_late, early, late), (near, half, 1)],
    )
    odd = plans(
        first_of[1],
        [(near, half - 1, 1), (keep_late, half, late), (keep_early, sectors - early, early)],
        [(carried_late, half, late), (carried_early, sectors - early, early), (far, sectors, 1)],
    )
    return even, odd


def pair_kernel(second, late, sectors, refs):
    half = sectors // 2
    early, next_early = chunk_sizes(half)
    part = next_early if second else early
    first_of = (part, half) if late else (0, sectors - part)
    table, partner_sizes = refs[:2]
    operand_count = 6 if second else 5
    operands = refs[2 : 2 + operand_count]
    sketch_ref = refs[2 + operand_count]
    outputs = refs[3 + operand_count : -9]
    (
        left_ref,
        right_ref,
        two_ref,
        sample_ref,
        gram_ref,
        inverse_ref,
        rows_ref,
        square_ref,
        in_semaphores,
    ) = refs[-9:]
    send, keep, norm_ref, *extras = outputs
    count, kept, double = sample_ref.shape
    width = double // 2
    plans = second_plans if second else first_plans
    run_by_parity(*plans(first_of, count, half, early, operands, left_ref, right_ref), in_semaphores)

    parity = lax.rem(lax.axis_index("chain"), 2)
    is_even = parity == 0
    first = lax.axis_index("block") * sectors + jnp.where(is_even, *first_of)
    bond = parity if second else 1 - parity
    total = table.shape[1]

    def size_of(row, sector):
        return table[row, sector].astype(jnp.int32)


    def left_size(sector):
        at = jnp.clip(sector, 0, total - 1)
        return jnp.where(is_even, size_of(0, at), partner_sizes[0, 0, at])

    def middle_size(sector):
        at = jnp.clip(sector, 0, total - 1)
        size = size_of(jnp.where(is_even, 1, 0), at)
        return jnp.where(sector < total, size, 0)

    def right_size(sector):
        at = jnp.clip(sector, 0, total - 1)
        size = jnp.where(is_even, partner_sizes[0, 1, at], size_of(1, at))
        return jnp.where(sector < total, size, 0)

    row_index = lax.broadcasted_iota(jnp.int32, (kept, 1), 0)
    eye = (
        lax.broadcasted_iota(jnp.int32, (kept, kept), 0)
        == lax.broadcasted_iota(jnp.int32, (kept, kept), 1)
    )
    block_row = lax.broadcasted_iota(jnp.int32, (width, width), 0)
    block_column = lax.broadcasted_iota(jnp.int32, (width, width), 1)
    column = lax.broadcasted_iota(jnp.int32, (1, width), 1)

    def left(m, s, sector):
        if second:
            return left_ref[m, :, s * width : (s + 1) * width]
        inside = (column < middle_size(sector + s)).astype(jnp.float32).astype(jnp.bfloat16)
        return left_ref[m, s] * inside

    def right(m, s):
        if second:
            return right_ref[m, :, s * width : (s + 1) * width]
        return right_ref[m, s]

    def product(a, b):
        rounded = dot(a, b, LAST if second else PLAIN).astype(jnp.bfloat16)
        return rounded.astype(jnp.float32)

    def put(m, rows, columns, value, row_limit, column_limit):
        if not second:
            value = jnp.where(
                (block_row < row_limit) & (block_column < column_limit), value, 0.0
            )
        two_ref[m, rows, columns] = value.astype(jnp.bfloat16)

    w_empty, w_stay, w_swap, w_full = gate_terms(
        *(jnp.full((1, width), table[4 + bond, term], jnp.float32) for term in range(3))
    )

    @pl.loop(0, count, unroll=min(UNROLL, count))
    def _(m):
        sector = first + m
        below_zero, below_one = left(m, 0, sector - 1), left(m, 1, sector - 1)
        here_zero, here_one = left(m + 1, 0, sector), left(m + 1, 1, sector)
        same_zero, same_one = right(m, 0), right(m, 1)
        next_zero, next_one = right(m + 1, 0), right(m + 1, 1)
        low, high = slice(0, width), slice(width, double)
        rows_low, rows_high = left_size(sector), left_size(sector - 1)
        columns_low, columns_high = right_size(sector), right_size(sector + 1)
        put(m, low, low, w_empty * product(here_zero, same_zero), rows_low, columns_low)
        put(
            m,
            low,
            high,
            w_stay * product(here_zero, next_one) + w_swap * product(here_one, next_zero),
            rows_low,
            columns_high,
        )
        put(
            m,
            high,
            low,
            w_swap * product(below_zero, same_one) + w_stay * product(below_one, same_zero),
            rows_high,
            columns_low,
        )
        put(m, high, high, w_full * product(below_one, next_one), rows_high, columns_high)
        sample = dot(sketch_ref[...], two_ref[m], LAST)
        keep_rows = row_index < size_of(2 + bond, sector)
        sample = jnp.where(keep_rows, sample, 0.0)
        sample_ref[m] = sample
        high_part, middle_part, low_part = in_parts(sample)
        cross = dot(high_part, middle_part, LAST) + dot(high_part, low_part, LAST)
        gram = dot(high_part, high_part, LAST) + (
            dot(middle_part, middle_part, LAST) + (cross + jnp.transpose(cross))
        )
        gram_ref[m] = gram + jnp.where(eye & jnp.logical_not(keep_rows), 1.0, 0.0)

    lane = lax.broadcasted_iota(jnp.int32, (1, kept), 1)
    def eliminate(tile, first, below):
        here = pl.ds(first, PANEL)
        stop = first + PANEL
        for m in range(count):
            for half in range(kept // LANES):
                span = slice(half * LANES, (half + 1) * LANES)
                rows_ref[half, pl.ds(m, PANEL, stride=SUB), :] = gram_ref[m, here, span]
        factor_panel(rows_ref, first, tile)
        for m in range(count):
            solved = jnp.concatenate(
                [
                    rows_ref[half, pl.ds(m, PANEL, stride=SUB), :]
                    for half in range(kept // LANES)
                ],
                axis=1,
            )
            inverse_ref[m, here, :] = jnp.where(lane < stop, solved, 0.0)
            if below.start == kept:
                continue
            high, middle, low = in_parts(solved)
            one = jnp.concatenate([high, high, middle, middle, high, low], axis=0)[:, below]
            two = jnp.concatenate([high, middle, high, middle, low, high], axis=0)
            change = dot(one, two, FIRST)
            kept_part = jnp.where((lane >= first) & (lane < stop), 0.0, gram_ref[m, below, :])
            gram_ref[m, below, :] = kept_part - change

    for tile in range(kept // LANES):
        if second and late:
            for first in range(tile * LANES, (tile + 1) * LANES, PANEL):
                stop = first + PANEL
                eliminate(tile, first, slice(stop - stop % LANES, kept))
        else:

            @pl.loop(0, LANES // PANEL)
            def _(panel, tile=tile):
                first = pl.multiple_of(tile * LANES + panel * PANEL, PANEL)
                eliminate(tile, first, slice(tile * LANES, kept))

    square_ref[...] = jnp.zeros_like(square_ref)

    @pl.loop(0, count, unroll=min(UNROLL, count))
    def _(m):
        inverse_high, inverse_middle, _ = in_parts(inverse_ref[m])
        sample_high, sample_middle, _ = in_parts(sample_ref[m])
        solved = dot(inverse_high, sample_high, PLAIN) + (
            dot(inverse_high, sample_middle, PLAIN) + dot(inverse_middle, sample_high, PLAIN)
        )
        solved = solved * math.sqrt(width)
        basis = solved.astype(jnp.bfloat16)
        coef = dot(basis, two_ref[m], PLAIN)
        square_ref[...] += jnp.sum(coef * coef, axis=0, keepdims=True)
        if second:
            for s in range(2):
                span = slice(s * width, (s + 1) * width)
                turned = jnp.transpose(solved[:, span])
                send[m, s] = jnp.where(is_even, turned, coef[:, span]).astype(jnp.bfloat16)
                keep[m, s] = jnp.where(is_even, coef[:, span], turned).astype(jnp.bfloat16)
        else:
            send[m] = jnp.where(is_even, coef, solved).astype(jnp.bfloat16)
            keep[m] = jnp.where(is_even, solved, coef).astype(jnp.bfloat16)

    norm_ref[0] = jnp.sum(square_ref[...])
    if second:
        if extras:
            extras[0][0] = send[0, 1]
    else:
        at = jnp.where(is_even, count - 1, 0) if late else jnp.where(is_even, 0, count - 1)
        extras[0][0] = send[at] if late else keep[at]


def pair_update(second, late, table, partner_sizes, operands, sketch_turned):
    kept, double = sketch_turned.shape
    width = double // 2
    sectors = table.shape[1] // lax.axis_size("block")
    half = sectors // 2
    early, next_early = chunk_sizes(half)
    part = next_early if second else early
    count = half - part if late else part
    block = (2, width, kept) if second else (kept, double)
    extra = [(1, kept, double)]
    if second:
        extra = [(1, width, kept)] if not late or next_early == 0 else []
    left_shape = (count + 1, kept, double) if second else (count + 1, 2, width, width)
    vmem = pl.BlockSpec(memory_space=pltpu.VMEM)
    smem = pl.BlockSpec(memory_space=pltpu.SMEM)
    anywhere = pl.BlockSpec(memory_space=pl.ANY)

    def kernel(*refs):
        pair_kernel(second, late, sectors, refs)

    return pl.pallas_call(
        kernel,
        out_shape=[
            jax.ShapeDtypeStruct((count, *block), jnp.bfloat16),
            jax.ShapeDtypeStruct((count, *block), jnp.bfloat16),
            jax.ShapeDtypeStruct((1,), jnp.float32),
            *(jax.ShapeDtypeStruct(shape, jnp.bfloat16) for shape in extra),
        ],
        in_specs=[smem] * 2 + [anywhere] * len(operands) + [vmem],
        out_specs=[vmem, vmem, smem] + [vmem] * len(extra),
        scratch_shapes=[
            pltpu.VMEM(left_shape, jnp.bfloat16),
            pltpu.VMEM(left_shape, jnp.bfloat16),
            pltpu.VMEM((count, double, double), jnp.bfloat16),
            pltpu.VMEM((count, kept, double), jnp.float32),
            pltpu.VMEM((count, kept, kept), jnp.float32),
            pltpu.VMEM((count, kept, kept), jnp.float32),
            pltpu.VMEM((kept // LANES, PANEL * SUB, LANES), jnp.float32),
            pltpu.VMEM((1, double), jnp.float32),
            pltpu.SemaphoreType.DMA((8,)),
        ],
        compiler_params=pltpu.CompilerParams(vmem_limit_bytes=32 * 2**20),
        cost_estimate=pl.CostEstimate(
            flops=(count + 12) * 50 * kept * double * double,
            bytes_accessed=8 * count * kept * double * 2,
            transcendentals=0,
        ),
    )(table, partner_sizes, *operands, sketch_turned)


def place_kernel(half, target, norm_refs, refs):
    _, early = chunk_sizes(half)
    late, sectors = half - early, 2 * half
    keep_late, returned_late, lower = refs[:3]
    even_line = [(keep_late, early, late), (returned_late, half, late)]
    odd_line = [(returned_late, early, late), (keep_late, half, late)]
    if early:
        keep_early, returned_early = refs[3:5]
        even_line += [(keep_early, 0, early), (returned_early, sectors - early, early)]
        odd_line += [(returned_early, 0, early), (keep_early, sectors - early, early)]
    lower_line = [(whole(lower), sectors, 1)]
    out, buffer, in_semaphores, out_semaphores = refs[-4:]
    site = out.at[0]
    zero_line = [(plane(ref, 0), start, size) for ref, start, size in odd_line]
    one_line = [(plane(ref, 1), start, size) for ref, start, size in odd_line]
    odd = cut(zero_line, 0, sectors, plane(site, 0))
    odd += cut(one_line + lower_line, 1, sectors, plane(site, 1))
    parts = even_line
    is_even = lax.rem(lax.axis_index("chain"), 2) == 0

    @pl.when(jnp.logical_not(is_even))
    def _():
        run_copies(odd, out_semaphores)

    @pl.when(is_even)
    def _():
        norms, from_left, direct = norm_refs
        rows = (1, buffer.shape[-1])
        norm_even = jnp.full(rows, from_left[0] + direct[0], jnp.float32)
        norm_odd = jnp.full(rows, norms[1] + from_left[1], jnp.float32)
        scale_even = jnp.sqrt(target / norm_even)
        scale = scale_even * jnp.sqrt(target / (scale_even * scale_even * norm_odd))
        coming, going, filled = [], [], 0
        for index, (source, start, size) in enumerate(parts):
            room = buffer.at[pl.ds(filled, size)]
            coming.append(pltpu.make_async_copy(source, room, in_semaphores.at[index]))
            going.append(
                pltpu.make_async_copy(room, out.at[0, pl.ds(start, size)], out_semaphores.at[index])
            )
            filled += size
        for copy in coming:
            copy.start()
        filled = 0
        for index, (source, start, size) in enumerate(parts):
            coming[index].wait()

            @pl.loop(filled, filled + size)
            def _(sector):
                for s in range(2):
                    scaled = buffer[sector, s].astype(jnp.float32) * scale
                    buffer[sector, s] = scaled.astype(jnp.bfloat16)

            going[index].start()
            filled += size
        for copy in going:
            copy.wait()


def place(half, target, norms, operands, site):
    anywhere = pl.BlockSpec(memory_space=pl.ANY)
    rows = 2 * half

    def kernel(*refs):
        place_kernel(half, target, refs[:3], refs[3:])

    return pl.pallas_call(
        kernel,
        out_shape=jax.ShapeDtypeStruct(site.shape, site.dtype),
        in_specs=[pl.BlockSpec(memory_space=pltpu.SMEM)] * 3 + [anywhere] * len(operands),
        out_specs=anywhere,
        scratch_shapes=[
            pltpu.VMEM((rows, *site.shape[2:]), site.dtype),
            pltpu.SemaphoreType.DMA((4,)),
            pltpu.SemaphoreType.DMA((9,)),
        ],
        compiler_params=pltpu.CompilerParams(vmem_limit_bytes=16 * 2**20),
        cost_estimate=pl.CostEstimate(
            flops=0, bytes_accessed=2 * rows * site.size // site.shape[1] * 2, transcendentals=0
        ),
    )(*norms, *operands)


def move(value, target_of):
    sites, parts = lax.axis_size("chain"), lax.axis_size("block")
    pairs = []
    for site in range(sites):
        for part in range(parts):
            target = target_of(site, part)
            if target is not None and 0 <= target[1] < parts:
                pairs.append((site * parts + part, (target[0] % sites) * parts + target[1]))
    return lax.ppermute(value, ("chain", "block"), pairs)


def by_parity(even_target, odd_target):
    return lambda c, b: even_target(c, b) if c % 2 == 0 else odd_target(c, b)


def nowhere(c, b):
    return None


def joined(*parts):
    return jnp.concatenate(parts, axis=0)


def body(site_tensors, sketch, bond_sizes, kept_ranks, couplings):
    sectors = site_tensors.shape[1]
    half = sectors // 2
    early, next_early = chunk_sizes(half)
    width = site_tensors.shape[-1]
    kept = sketch.shape[1]
    parts = lax.axis_size("block")
    is_even = lax.axis_index("chain") % 2 == 0
    own = site_tensors[0]
    sketch_turned = jnp.transpose(sketch)

    terms = jnp.pad(couplings[0], ((0, 0), (0, bond_sizes.shape[2] - couplings.shape[2])))
    table = joined(
        bond_sizes[0].astype(jnp.float32), kept_ranks[0].astype(jnp.float32), terms
    )

    def pick(even_value, odd_value):
        return jnp.where(is_even, even_value, odd_value)

    def update(second, late, *operands):
        return pair_update(
            second, late, table, partner_sizes, operands, sketch_turned
        )

    across = by_parity(lambda c, b: (c + 1, b), lambda c, b: (c - 1, b))
    got_early = move(pick(own[sectors - early - 1 :], own[: early + 1]), across)
    partner_sizes = move(bond_sizes, across)
    edge = move(
        pick(own[-1:], own[:1]), by_parity(lambda c, b: (c, b + 1), lambda c, b: (c, b - 1))
    )
    corner = move(own[-1:, 1], by_parity(nowhere, lambda c, b: (c - 1, b + 1)))
    sent = pick(own[half - 1 : sectors - early - 1], own[early + 1 : half + 1])
    own_early = pick(own[: early + 1], own[sectors - early - 1 :])
    own_late = pick(own[early - 1 : half + 1], own[half - 1 : sectors - early + 1])
    sent, got_early = lax.optimization_barrier((sent, got_early))
    got_late = move(sent, across)
    send_early, keep_early, norm_early, halo_early = update(
        False, False, own_early, got_early, got_early, edge, corner
    )

    along = by_parity(lambda c, b: (c + 2, b), lambda c, b: (c - 2, b))
    far = move(
        halo_early, by_parity(lambda c, b: (c - 1, b - 1), lambda c, b: (c + 1, b + 1))
    )
    carried_early = move(send_early, along)
    send_late, keep_late, norm_late, halo_late = update(
        False, True, own_late, got_early, got_late, edge, corner
    )
    norm_even = norm_early + norm_late
    carried_late = move(send_late, along)
    near = move(halo_late, across)

    back = by_parity(lambda c, b: (c - 1, b), lambda c, b: (c + 1, b))
    norm_odd = 0.0
    first_parts = ()
    if next_early:
        send_early, kept_early, norm_early, lower_first = update(
            True, False, keep_early, keep_early, carried_early, carried_early, far, far
        )
        norm_odd = norm_early
        send_early, carried_late = lax.optimization_barrier((send_early, carried_late))
        returned_early = move(send_early, back)
        first_parts = (kept_early, returned_early)
    send_late, kept_late, norm_late, *lower = update(
        True, True, keep_early, keep_late, carried_early, carried_late, far, near
    )
    if next_early == 0:
        lower_first = lower[0]
    lower_above = move(lower_first, by_parity(lambda c, b: (c - 1, b - 1), nowhere))
    if next_early:
        send_late, returned_early, lower_above = lax.optimization_barrier(
            (send_late, returned_early, lower_above)
        )
        first_parts = (kept_early, returned_early)
    returned_late = move(send_late, back)

    norms = lax.psum(joined(norm_even, norm_odd + norm_late), "block")
    hops = {1: 2, 3: -1}
    passed = move(norms, lambda c, b: (c + hops[c % 4], b) if c % 2 else None)
    direct = move(norms, lambda c, b: (c + 2, b) if c % 4 == 0 else None)
    mine = (lax.axis_index("chain") % 4 == 2) & (jnp.arange(2) == 0)
    hops_on = {3: -1, 2: 2}
    from_left = move(
        passed + jnp.where(mine, norms, 0.0),
        lambda c, b: (c + hops_on[c % 4], b) if c % 4 in hops_on else None,
    )
    target = float(sectors * parts * kept * width)
    norms = (norms, from_left, direct)

    ready = (kept_late, returned_late, lower_above, *first_parts)
    return place(half, target, norms, ready, site_tensors)


def solution(mesh):
    placed = (
        P("chain", "block", None, None, None),
        P(),
        P("chain", None, None),
        P("chain", None, None),
        P("chain", None, None),
    )
    return jax.shard_map(
        body,
        mesh=mesh,
        in_specs=placed,
        out_specs=P("chain", "block", None, None, None),
        check_vma=False,
    )
```

profile of v0, /device:TPU:0, one launch (start us, length us, event | category | flops | bytes accessed | tf_op | source)
XLA Modules:
  0.0 179.1 jit_solution(5025753587984492818)
XLA Ops:
  0.0 2.9 %collective-permute-start = (s32[1,2,32]{2,1,0:T(2,128)}, s32[1,2,32]{2,1,0:T(2,128)S(1)}, u32[]{:S(2)}, u32[]{:S(2)}) collective-permute-start(s32[1,2,32]{2,1,0:T(2,128)} %param.7), channel_id=1, source_target_pairs={{0,2},{1,3},{2,0},{3,1},{4,6},{5,7},{6,4},{7,5},{8,10},{9,11},{10,... | collective-permute-start | bytes 776 | tf_op jit(solution)/shard_map/ppermute | solution.py:536
  2.9 3.1 %select_bitcast_fusion.1 = (bf16[5,2,256,256]{3,2,1,0:T(8,128)(2,1)}, bf16[5,2,256,256]{3,2,1,0:T(8,128)(2,1)S(1)}) fusion(pred[]{:T(512)S(6)} %eq.12, bf16[1,16,2,256,256]{4,3,2,1,0:T(8,128)(2,1)} %param.5), kind=kLoop, calls=%fused_computation.1 | loop fusion | flops 1310720 | bytes 5242881 | tf_op jit(solution)/shard_map/jit(_where)/select_n | solution.py:568
  8.1 2.1 %collective-permute-start.2 = (bf16[1,2,256,256]{3,2,1,0:T(8,128)(2,1)}, bf16[1,2,256,256]{3,2,1,0:T(8,128)(2,1)S(1)}, u32[]{:S(2)}, u32[]{:S(2)}) collective-permute-start(bf16[1,2,256,256]{3,2,1,0:T(8,128)(2,1)} %select_bitcast_fusion.4), channel_id=1, source_target_pairs={{0,1},{3,2},{4,5},{7,6},{8,9},{11,10},{12,13},{15,14},{16,17},{19,... | collective-permute-start | bytes 786440 | tf_op jit(solution)/shard_map/ppermute | solution.py:536
  10.2 1.1 select_bitcast_fusion.3
  12.0 1.1 copy.6
  13.1 23.5 %collective-permute-done.1.refs_3_.refs_4_ = bf16[5,2,256,256]{3,2,1,0:T(8,128)(2,1)} collective-permute-done((bf16[5,2,256,256]{3,2,1,0:T(8,128)(2,1)}, bf16[5,2,256,256]{3,2,1,0:T(8,128)(2,1)}, u32[]{:S(2)}, u32[]{:S(2)}) %collective-permute-start.1) | collective-permute-done | bytes 1310752 | tf_op jit(solution)/shard_map/ppermute | solution.py:536
  36.9 21.5 %shard_map.55 = (bf16[4,256,512]{2,1,0:T(8,128)(2,1)S(1)}, bf16[4,256,512]{2,1,0:T(8,128)(2,1)S(1)}, f32[1]{0:T(128)}, bf16[1,256,512]{2,1,0:T(8,128)(2,1)S(1)}) custom-call(f32[6,32]{1,0:T(8,128)S(1)} %select_maximum_fusion.refs_0_, s32[1,2,32]{2,1,0:T(2,128)S(1)} %collective-permute-done.refs_1_, bf16[5,2,256,256]{3,2,1,0:T(8,128)(2,1)S(1)} %get-tuple-element.50.refs_2_, ...), custom_call_target="tpu_custom_call" | custom-call | flops 53687091200 | bytes 8388608 | tf_op jit(solution)/shard_map/pallas_call | solution.py:416
  59.0 1.8 %collective-permute-start.5 = (bf16[4,256,512]{2,1,0:T(8,128)(2,1)S(1)}, bf16[4,256,512]{2,1,0:T(8,128)(2,1)S(1)}, u32[]{:S(2)}, u32[]{:S(2)}) collective-permute-start(bf16[4,256,512]{2,1,0:T(8,128)(2,1)S(1)} %get-tuple-element.32), channel_id=1, source_target_pairs={{0,4},{1,5},{2,30},{3,31},{4,8},{5,9},{6,2},{7,3},{8,12},{9,13},{1... | collective-permute-start | bytes 3145736 | tf_op jit(solution)/shard_map/ppermute | solution.py:536
  60.9 21.3 %shard_map.56 = (bf16[4,256,512]{2,1,0:T(8,128)(2,1)S(1)}, bf16[4,256,512]{2,1,0:T(8,128)(2,1)S(1)}, f32[1]{0:T(128)}, bf16[1,256,512]{2,1,0:T(8,128)(2,1)S(1)}) custom-call(f32[6,32]{1,0:T(8,128)S(1)} %select_maximum_fusion.refs_0_, s32[1,2,32]{2,1,0:T(2,128)S(1)} %collective-permute-done.refs_1_, bf16[6,2,256,256]{3,2,1,0:T(8,128)(2,1)S(1)} %select_bitcast_fusion.refs_2_, ...), custom_call_target="tpu_custom_call" | custom-call | flops 53687091200 | bytes 8388608 | tf_op jit(solution)/shard_map/pallas_call | solution.py:416
  82.1 6.0 %collective-permute-start.8 = (bf16[1,256,512]{2,1,0:T(8,128)(2,1)S(1)}, bf16[1,256,512]{2,1,0:T(8,128)(2,1)S(1)}, u32[]{:S(2)}, u32[]{:S(2)}) collective-permute-start(bf16[1,256,512]{2,1,0:T(8,128)(2,1)S(1)} %get-tuple-element.39), channel_id=1, source_target_pairs={{0,2},{1,3},{2,0},{3,1},{4,6},{5,7},{6,4},{7,5},{8,10},{9,11},{10,... | collective-permute-start | bytes 786440 | tf_op jit(solution)/shard_map/ppermute | solution.py:536
  88.2 0.9 copy-done.3
  89.2 18.3 %shard_map.57 = (bf16[3,2,256,256]{3,2,1,0:T(8,128)(2,1)S(1)}, bf16[3,2,256,256]{3,2,1,0:T(8,128)(2,1)S(1)}, f32[1]{0:T(128)}, bf16[1,256,256]{2,1,0:T(8,128)(2,1)S(1)}) custom-call(f32[6,32]{1,0:T(8,128)S(1)} %select_maximum_fusion.refs_0_, s32[1,2,32]{2,1,0:T(2,128)S(1)} %collective-permute-done.refs_1_, ...), custom_call_target="tpu_custom_call" | custom-call | flops 50331648000 | bytes 6291456 | tf_op jit(solution)/shard_map/pallas_call | solution.py:416
  108.2 7.2 %collective-permute-done.7.refs_5_ = bf16[4,256,512]{2,1,0:T(8,128)(2,1)S(1)} collective-permute-done((bf16[4,256,512]{2,1,0:T(8,128)(2,1)S(1)}, bf16[4,256,512]{2,1,0:T(8,128)(2,1)S(1)}, u32[]{:S(2)}, u32[]{:S(2)}) %collective-permute-start.7) | collective-permute-done | bytes 1048608 | tf_op jit(solution)/shard_map/ppermute | solution.py:536
  115.6 21.4 %shard_map.58 = (bf16[5,2,256,256]{3,2,1,0:T(8,128)(2,1)}, bf16[5,2,256,256]{3,2,1,0:T(8,128)(2,1)S(1)}, f32[1]{0:T(128)}) custom-call(f32[6,32]{1,0:T(8,128)S(1)} %select_maximum_fusion.refs_0_, s32[1,2,32]{2,1,0:T(2,128)S(1)} %collective-permute-done.refs_1_, bf16[4,256,512]{2,1,0:T(8,128)(2,1)S(1)} %get-tuple-element.31.refs_2_.refs_3_, ...), custom_call_target="tpu_custom_call" | custom-call | flops 57042534400 | bytes 10485760 | tf_op jit(solution)/shard_map/pallas_call | solution.py:416
  137.0 1.2 collective-permute-done.12.refs_7_
  138.2 0.9 copy-done
  139.1 4.2 %collective-permute-start.14 = (bf16[5,2,256,256]{3,2,1,0:T(8,128)(2,1)}, bf16[5,2,256,256]{3,2,1,0:T(8,128)(2,1)S(1)}, u32[]{:S(2)}, u32[]{:S(2)}) collective-permute-start(bf16[5,2,256,256]{3,2,1,0:T(8,128)(2,1)} %get-tuple-element.45), channel_id=1, source_target_pairs={{0,30},{1,31},{2,4},{3,5},{4,2},{5,3},{6,8},{7,9},{8,6},{9,7},{10,... | collective-permute-start | bytes 3932168 | tf_op jit(solution)/shard_map/ppermute | solution.py:536
  145.9 2.4 %psum.7.refs_0_ = f32[2]{0:T(128)S(1)} all-reduce(f32[2]{0:T(128)S(1)} %pad_maximum_fusion), channel_id=1, replica_groups=mesh['chain'=16,'block'=2] {'block'}, use_global_device_ids=true, to_apply=%region_0.1 | all-reduce | flops 2 | bytes 16 | tf_op jit(solution)/shard_map/psum | solution.py:627
  148.3 1.3 collective-permute-start.11
  150.3 1.3 collective-permute-start.10
  151.6 6.8 %collective-permute-done.10.refs_1_ = f32[2]{0:T(128)S(1)} collective-permute-done((f32[2]{0:T(128)S(1)}, f32[2]{0:T(128)S(1)}, u32[]{:S(2)}, u32[]{:S(2)}) %collective-permute-start.10) | collective-permute-done | bytes 40 | tf_op jit(solution)/shard_map/ppermute | solution.py:536
  158.4 16.1 %collective-permute-done.14.refs_4_ = bf16[5,2,256,256]{3,2,1,0:T(8,128)(2,1)S(1)} collective-permute-done((bf16[5,2,256,256]{3,2,1,0:T(8,128)(2,1)}, bf16[5,2,256,256]{3,2,1,0:T(8,128)(2,1)S(1)}, u32[]{:S(2)}, u32[]{:S(2)}) %collective-permute-start.14) | collective-permute-done | bytes 1310752 | tf_op jit(solution)/shard_map/ppermute | solution.py:536
  174.6 1.1 copy-done.1
  175.7 3.2 %shard_map.59 = bf16[1,16,2,256,256]{4,3,2,1,0:T(8,128)(2,1)} custom-call(f32[2]{0:T(128)S(1)} %psum.7.refs_0_, f32[2]{0:T(128)S(1)} %collective-permute-done.10.refs_1_, f32[2]{0:T(128)S(1)} %collective-permute-done.11.refs_2_, bf16[5,2,256,256]{3,2,1,0:T(8,128)(2,1)S(1)} %get-tuple-element.41.refs_3_, ...), custom_call_target="tpu_custom_call" | custom-call | bytes 8388608 | tf_op jit(solution)/shard_map/pallas_call | solution.py:511
  (38 shorter events, 5.4 us)
Async XLA Ops:
  0.0 36.9 %collective-permute-start = (s32[1,2,32]{2,1,0:T(2,128)}, s32[1,2,32]{2,1,0:T(2,128)S(1)}, u32[]{:S(2)}, u32[]{:S(2)}) collective-permute-start(s32[1,2,32]{2,1,0:T(2,128)} %param.7), channel_id=1, source_target_pairs={{0,2},{1,3},{2,0},{3,1},{4,6},{5,7},{6,4},{7,5},{8,10},{9,11},{10,... | collective-permute-start | bytes 776 | tf_op jit(solution)/shard_map/ppermute | solution.py:536
  2.9 3.1 %copy-start.4 = (bf16[1,16,2,256,256]{4,3,2,1,0:T(8,128)(2,1)S(1)}, bf16[1,16,2,256,256]{4,3,2,1,0:T(8,128)(2,1)}, u32[]{:S(2)}) copy-start(bf16[1,16,2,256,256]{4,3,2,1,0:T(8,128)(2,1)} %param.5) | copy-start | bytes 12582916
  6.0 30.6 %collective-permute-start.1 = (bf16[5,2,256,256]{3,2,1,0:T(8,128)(2,1)}, bf16[5,2,256,256]{3,2,1,0:T(8,128)(2,1)}, u32[]{:S(2)}, u32[]{:S(2)}) collective-permute-start(bf16[5,2,256,256]{3,2,1,0:T(8,128)(2,1)} %get-tuple-element.49), channel_id=1, source_target_pairs={{0,2},{1,3},{2,0},{3,1},{4,6},{5,7},{6,4},{7,5},{8,10},{9,11},{10,... | collective-permute-start | bytes 3932168 | tf_op jit(solution)/shard_map/ppermute | solution.py:536
  6.7 30.2 %collective-permute-start.3 = (bf16[1,256,256]{2,1,0:T(8,128)(2,1)}, bf16[1,256,256]{2,1,0:T(8,128)(2,1)S(1)}, u32[]{:S(2)}, u32[]{:S(2)}) collective-permute-start(bf16[1,256,256]{2,1,0:T(8,128)(2,1)} %slice_bitcast_fusion), channel_id=1, source_target_pairs={{2,1},{6,5},{10,9},{14,13},{18,17},{22,21},{26,25},{30,29}} | collective-permute-start | bytes 393224 | tf_op jit(solution)/shard_map/ppermute | solution.py:536
  8.1 28.8 %collective-permute-start.2 = (bf16[1,2,256,256]{3,2,1,0:T(8,128)(2,1)}, bf16[1,2,256,256]{3,2,1,0:T(8,128)(2,1)S(1)}, u32[]{:S(2)}, u32[]{:S(2)}) collective-permute-start(bf16[1,2,256,256]{3,2,1,0:T(8,128)(2,1)} %select_bitcast_fusion.4), channel_id=1, source_target_pairs={{0,1},{3,2},{4,5},{7,6},{8,9},{11,10},{12,13},{15,14},{16,17},{19,... | collective-permute-start | bytes 786440 | tf_op jit(solution)/shard_map/ppermute | solution.py:536
  11.3 0.7 copy-start.6
  11.3 0.7 copy-start.7
  11.3 1.8 %copy-start.5 = (f32[1,2,3]{2,1,0:T(2,128)S(1)}, f32[1,2,3]{2,1,0:T(2,128)}, u32[]{:S(2)}) copy-start(f32[1,2,3]{2,1,0:T(2,128)} %param.9) | copy-start | bytes 76
  13.1 47.8 %copy-start.2 = (bf16[512,256]{0,1:T(8,128)(2,1)}, bf16[512,256]{0,1:T(8,128)(2,1)S(1)}, u32[]{:S(2)}) copy-start(bf16[512,256]{0,1:T(8,128)(2,1)S(1)} %copy.6) | copy-start | bytes 786436
  36.6 24.3 %collective-permute-start.4 = (bf16[4,2,256,256]{3,2,1,0:T(8,128)(2,1)}, bf16[4,2,256,256]{3,2,1,0:T(8,128)(2,1)S(1)}, u32[]{:S(2)}, u32[]{:S(2)}) collective-permute-start(bf16[4,2,256,256]{3,2,1,0:T(8,128)(2,1)} %select_bitcast_fusion.3), channel_id=1, source_target_pairs={{0,2},{1,3},{2,0},{3,1},{4,6},{5,7},{6,4},{7,5},{8,10},{9,11},{10,... | collective-permute-start | bytes 3145736 | tf_op jit(solution)/shard_map/ppermute | solution.py:536
  58.4 29.8 %collective-permute-start.6 = (bf16[1,256,512]{2,1,0:T(8,128)(2,1)S(1)}, bf16[1,256,512]{2,1,0:T(8,128)(2,1)S(1)}, u32[]{:S(2)}, u32[]{:S(2)}) collective-permute-start(bf16[1,256,512]{2,1,0:T(8,128)(2,1)S(1)} %get-tuple-element.33), channel_id=1, source_target_pairs={{1,30},{2,5},{5,2},{6,9},{9,6},{10,13},{13,10},{14,17},{17,14},{18... | collective-permute-start | bytes 786440 | tf_op jit(solution)/shard_map/ppermute | solution.py:536
  59.0 29.2 %collective-permute-start.5 = (bf16[4,256,512]{2,1,0:T(8,128)(2,1)S(1)}, bf16[4,256,512]{2,1,0:T(8,128)(2,1)S(1)}, u32[]{:S(2)}, u32[]{:S(2)}) collective-permute-start(bf16[4,256,512]{2,1,0:T(8,128)(2,1)S(1)} %get-tuple-element.32), channel_id=1, source_target_pairs={{0,4},{1,5},{2,30},{3,31},{4,8},{5,9},{6,2},{7,3},{8,12},{9,13},{1... | collective-permute-start | bytes 3145736 | tf_op jit(solution)/shard_map/ppermute | solution.py:536
  82.1 33.5 %collective-permute-start.8 = (bf16[1,256,512]{2,1,0:T(8,128)(2,1)S(1)}, bf16[1,256,512]{2,1,0:T(8,128)(2,1)S(1)}, u32[]{:S(2)}, u32[]{:S(2)}) collective-permute-start(bf16[1,256,512]{2,1,0:T(8,128)(2,1)S(1)} %get-tuple-element.39), channel_id=1, source_target_pairs={{0,2},{1,3},{2,0},{3,1},{4,6},{5,7},{6,4},{7,5},{8,10},{9,11},{10,... | collective-permute-start | bytes 786440 | tf_op jit(solution)/shard_map/ppermute | solution.py:536
  88.2 27.2 %collective-permute-start.7 = (bf16[4,256,512]{2,1,0:T(8,128)(2,1)S(1)}, bf16[4,256,512]{2,1,0:T(8,128)(2,1)S(1)}, u32[]{:S(2)}, u32[]{:S(2)}) collective-permute-start(bf16[4,256,512]{2,1,0:T(8,128)(2,1)S(1)} %get-tuple-element.37), channel_id=1, source_target_pairs={{0,4},{1,5},{2,30},{3,31},{4,8},{5,9},{6,2},{7,3},{8,12},{9,13},{1... | collective-permute-start | bytes 3145736 | tf_op jit(solution)/shard_map/ppermute | solution.py:536
  88.2 1.0 copy-start.3
  107.5 29.5 %collective-permute-start.13 = (bf16[1,256,256]{2,1,0:T(8,128)(2,1)S(1)}, bf16[1,256,256]{2,1,0:T(8,128)(2,1)S(1)}, u32[]{:S(2)}, u32[]{:S(2)}) collective-permute-start(bf16[1,256,256]{2,1,0:T(8,128)(2,1)S(1)} %get-tuple-element.44), channel_id=1, source_target_pairs={{1,30},{5,2},{9,6},{13,10},{17,14},{21,18},{25,22},{29,26}} | collective-permute-start | bytes 393224 | tf_op jit(solution)/shard_map/ppermute | solution.py:536
  115.4 22.9 %collective-permute-start.12 = (bf16[3,2,256,256]{3,2,1,0:T(8,128)(2,1)S(1)}, bf16[3,2,256,256]{3,2,1,0:T(8,128)(2,1)S(1)}, u32[]{:S(2)}, u32[]{:S(2)}) collective-permute-start(bf16[3,2,256,256]{3,2,1,0:T(8,128)(2,1)S(1)} %get-tuple-element.43), channel_id=1, source_target_pairs={{0,30},{1,31},{2,4},{3,5},{4,2},{5,3},{6,8},{7,9},{8,6},{9,7},{10,... | collective-permute-start | bytes 2359304 | tf_op jit(solution)/shard_map/ppermute | solution.py:536
  138.2 0.9 copy-start
  139.1 35.4 %collective-permute-start.14 = (bf16[5,2,256,256]{3,2,1,0:T(8,128)(2,1)}, bf16[5,2,256,256]{3,2,1,0:T(8,128)(2,1)S(1)}, u32[]{:S(2)}, u32[]{:S(2)}) collective-permute-start(bf16[5,2,256,256]{3,2,1,0:T(8,128)(2,1)} %get-tuple-element.45), channel_id=1, source_target_pairs={{0,30},{1,31},{2,4},{3,5},{4,2},{5,3},{6,8},{7,9},{8,6},{9,7},{10,... | collective-permute-start | bytes 3932168 | tf_op jit(solution)/shard_map/ppermute | solution.py:536
  148.3 3.3 %collective-permute-start.11 = (f32[2]{0:T(128)S(1)}, f32[2]{0:T(128)S(1)}, u32[]{:S(2)}, u32[]{:S(2)}) collective-permute-start(f32[2]{0:T(128)S(1)} %psum.7.refs_0_), channel_id=1, source_target_pairs={{0,4},{1,5},{8,12},{9,13},{16,20},{17,21},{24,28},{25,29}} | collective-permute-start | bytes 32 | tf_op jit(solution)/shard_map/ppermute | solution.py:536
  149.6 0.7 collective-permute-start.9
  150.3 8.1 %collective-permute-start.10 = (f32[2]{0:T(128)S(1)}, f32[2]{0:T(128)S(1)}, u32[]{:S(2)}, u32[]{:S(2)}) collective-permute-start(f32[2]{0:T(128)S(1)} %fusion), channel_id=1, source_target_pairs={{4,8},{5,9},{6,4},{7,5},{12,16},{13,17},{14,12},{15,13},{20,24},{2... | collective-permute-start | bytes 32 | tf_op jit(solution)/shard_map/ppermute | solution.py:536
  174.6 1.1 copy-start.1
where the time goes:
time: 180 us; the launch traced here: 179 us
  Pallas kernels  85.7 us (48%)
  waiting for transfers between devices  54.9 us (30%)
  starting transfers between devices  22.8 us (13%)
  local copies, waits for them, and re-layouts  5.25 us (3%)
  other arithmetic  5.18 us (3%)
  between operations  2.81 us (2%)
  blocking collectives  2.44 us (1%)
    pallas_call x4, Pallas kernels, pair_update(): pl.pallas_call(kernel, out_shape=[jax.ShapeDtypeStruct((count, *block), j...  82.5 us
    ppermute x15, waiting for transfers between devices, move(): return lax.ppermute(value, ('chain', 'block'), pairs)  54.9 us
    ppermute x15, starting transfers between devices, move(): return lax.ppermute(value, ('chain', 'block'), pairs)  22.8 us
    select_n x4, other arithmetic, pick(): return jnp.where(is_even, even_value, odd_value)  5.08 us
    unnamed x17, local copies, waits for them, and re-layouts  4.59 us
  transfers between devices with their start and end apart: 15, of which 5 were waited for; matrix products, arithmetic and copies ran while one was open for 4% of the time, Pallas kernels for 46%

commit v1 on v0

--- a/solution.py
+++ b/solution.py
@@ -443,18 +443,24 @@
     )(table, partner_sizes, *operands, sketch_turned)
 
 
-def place_kernel(half, target, norm_refs, refs):
+def place_kernel(last, half, target, norm_refs, refs):
     _, early = chunk_sizes(half)
     late, sectors = half - early, 2 * half
-    keep_late, returned_late, lower = refs[:3]
-    even_line = [(keep_late, early, late), (returned_late, half, late)]
-    odd_line = [(returned_late, early, late), (keep_late, half, late)]
-    if early:
-        keep_early, returned_early = refs[3:5]
-        even_line += [(keep_early, 0, early), (returned_early, sectors - early, early)]
-        odd_line += [(returned_early, 0, early), (keep_early, sectors - early, early)]
-    lower_line = [(whole(lower), sectors, 1)]
-    out, buffer, in_semaphores, out_semaphores = refs[-4:]
+    if last:
+        returned_late, _, out, buffer, in_semaphores, out_semaphores = refs
+        even_line = [(returned_late, half, late)]
+        odd_line = [(returned_late, early, late)]
+        lower_line = []
+    else:
+        if early:
+            keep_late, lower, keep_early, returned_early = refs[:4]
+            even_line = [(keep_early, 0, early), (keep_late, early, late), (returned_early, sectors - early, early)]
+            odd_line = [(returned_early, 0, early), (keep_late, half, late), (keep_early, sectors - early, early)]
+        else:
+            keep_late, lower = refs[:2]
+            even_line, odd_line = [(keep_late, 0, late)], [(keep_late, half, late)]
+        lower_line = [(whole(lower), sectors, 1)]
+        out, buffer, in_semaphores, out_semaphores = refs[-4:]
     site = out.at[0]
     zero_line = [(plane(ref, 0), start, size) for ref, start, size in odd_line]
     one_line = [(plane(ref, 1), start, size) for ref, start, size in odd_line]
@@ -501,12 +507,13 @@
             copy.wait()
 
 
-def place(half, target, norms, operands, site):
+def place(last, half, target, norms, operands, site):
     anywhere = pl.BlockSpec(memory_space=pl.ANY)
-    rows = 2 * half
+    _, early = chunk_sizes(half)
+    rows = half - early if last else half + early
 
     def kernel(*refs):
-        place_kernel(half, target, refs[:3], refs[3:])
+        place_kernel(last, half, target, refs[:3], refs[3:])
 
     return pl.pallas_call(
         kernel,
@@ -515,9 +522,10 @@
         out_specs=anywhere,
         scratch_shapes=[
             pltpu.VMEM((rows, *site.shape[2:]), site.dtype),
-            pltpu.SemaphoreType.DMA((4,)),
-            pltpu.SemaphoreType.DMA((9,)),
+            pltpu.SemaphoreType.DMA((3,)),
+            pltpu.SemaphoreType.DMA((7,)),
         ],
+        input_output_aliases={4: 0} if last else {},
         compiler_params=pltpu.CompilerParams(vmem_limit_bytes=16 * 2**20),
         cost_estimate=pl.CostEstimate(
             flops=0, bytes_accessed=2 * rows * site.size // site.shape[1] * 2, transcendentals=0
@@ -637,8 +645,9 @@
     target = float(sectors * parts * kept * width)
     norms = (norms, from_left, direct)
 
-    ready = (kept_late, returned_late, lower_above, *first_parts)
-    return place(half, target, norms, ready, site_tensors)
+    ready = (kept_late, lower_above, *first_parts)
+    site = place(False, half, target, norms, ready, site_tensors)
+    return place(True, half, target, norms, (returned_late, site), site_tensors)
 
 
 def solution(mesh):

time: 180 us -> 177 us (0.983)
  waiting for transfers between devices: 54.9 us -> 50.4 us
    ppermute x15, waiting for transfers between devices: 54.9 us -> 50.4 us  [move(): return lax.ppermute(value, ('chain', 'block'), pairs)]
    pallas_call x1 -> x2, Pallas kernels: 3.23 us -> 4.65 us  [place(): pl.pallas_call(kernel, out_shape=jax.ShapeDtypeStruct(site.shape, site.dt...]
  transfers between devices with their start and end apart: 15 -> 15, of which waited for: 5 -> 5; matrix products, arithmetic and copies ran while one was open for 4% -> 4% of each run, Pallas kernels for 46% -> 48%
where the time goes in v1:
time: 177 us
  Pallas kernels  87.4 us (49%)
  waiting for transfers between devices  50.4 us (28%)
  starting transfers between devices  23.1 us (13%)
  local copies, waits for them, and re-layouts  5.24 us (3%)
  other arithmetic  5.18 us (3%)
  between operations  2.86 us (2%)
  blocking collectives  2.44 us (1%)
    pallas_call x4, Pallas kernels, pair_update(): pl.pallas_call(kernel, out_shape=[jax.ShapeDtypeStruct((count, *block), j...  82.7 us
    ppermute x15, waiting for transfers between devices, move(): return lax.ppermute(value, ('chain', 'block'), pairs)  50.4 us
    ppermute x15, starting transfers between devices, move(): return lax.ppermute(value, ('chain', 'block'), pairs)  23.1 us
    select_n x4, other arithmetic, pick(): return jnp.where(is_even, even_value, odd_value)  5.08 us
    pallas_call x2, Pallas kernels, place(): pl.pallas_call(kernel, out_shape=jax.ShapeDtypeStruct(site.shape, site.dt...  4.65 us
    unnamed x17, local copies, waits for them, and re-layouts  4.58 us
  transfers between devices with their start and end apart: 15, of which 5 were waited for; matrix products, arithmetic and copies ran while one was open for 4% of the time, Pallas kernels for 48%

profile of v1, /device:TPU:0, one launch (start us, length us, event | category | flops | bytes accessed | tf_op | source)
XLA Modules:
  0.0 176.6 jit_solution(10993981212005870693)
XLA Ops:
  0.0 2.9 %collective-permute-start = (s32[1,2,32]{2,1,0:T(2,128)}, s32[1,2,32]{2,1,0:T(2,128)S(1)}, u32[]{:S(2)}, u32[]{:S(2)}) collective-permute-start(s32[1,2,32]{2,1,0:T(2,128)} %param.7), channel_id=1, source_target_pairs={{0,2},{1,3},{2,0},{3,1},{4,6},{5,7},{6,4},{7,5},{8,10},{9,11},{10,... | collective-permute-start | bytes 776 | tf_op jit(solution)/shard_map/ppermute | solution.py:544
  2.9 3.1 %select_bitcast_fusion.1 = (bf16[5,2,256,256]{3,2,1,0:T(8,128)(2,1)}, bf16[5,2,256,256]{3,2,1,0:T(8,128)(2,1)S(1)}) fusion(pred[]{:T(512)S(6)} %eq.12, bf16[1,16,2,256,256]{4,3,2,1,0:T(8,128)(2,1)} %param.5), kind=kLoop, calls=%fused_computation.1 | loop fusion | flops 1310720 | bytes 5242881 | tf_op jit(solution)/shard_map/jit(_where)/select_n | solution.py:576
  8.1 2.1 %collective-permute-start.2 = (bf16[1,2,256,256]{3,2,1,0:T(8,128)(2,1)}, bf16[1,2,256,256]{3,2,1,0:T(8,128)(2,1)S(1)}, u32[]{:S(2)}, u32[]{:S(2)}) collective-permute-start(bf16[1,2,256,256]{3,2,1,0:T(8,128)(2,1)} %select_bitcast_fusion.4), channel_id=1, source_target_pairs={{0,1},{3,2},{4,5},{7,6},{8,9},{11,10},{12,13},{15,14},{16,17},{19,... | collective-permute-start | bytes 786440 | tf_op jit(solution)/shard_map/ppermute | solution.py:544
  10.2 1.1 select_bitcast_fusion.3
  12.0 1.1 copy.7
  13.1 23.5 %collective-permute-done.1.refs_3_.refs_4_ = bf16[5,2,256,256]{3,2,1,0:T(8,128)(2,1)} collective-permute-done((bf16[5,2,256,256]{3,2,1,0:T(8,128)(2,1)}, bf16[5,2,256,256]{3,2,1,0:T(8,128)(2,1)}, u32[]{:S(2)}, u32[]{:S(2)}) %collective-permute-start.1) | collective-permute-done | bytes 1310752 | tf_op jit(solution)/shard_map/ppermute | solution.py:544
  36.9 21.5 %shard_map.55 = (bf16[4,256,512]{2,1,0:T(8,128)(2,1)S(1)}, bf16[4,256,512]{2,1,0:T(8,128)(2,1)S(1)}, f32[1]{0:T(128)}, bf16[1,256,512]{2,1,0:T(8,128)(2,1)S(1)}) custom-call(f32[6,32]{1,0:T(8,128)S(1)} %select_maximum_fusion.refs_0_, s32[1,2,32]{2,1,0:T(2,128)S(1)} %collective-permute-done.refs_1_, bf16[5,2,256,256]{3,2,1,0:T(8,128)(2,1)S(1)} %get-tuple-element.50.refs_2_, ...), custom_call_target="tpu_custom_call" | custom-call | flops 53687091200 | bytes 8388608 | tf_op jit(solution)/shard_map/pallas_call | solution.py:416
  59.1 1.8 %collective-permute-start.5 = (bf16[4,256,512]{2,1,0:T(8,128)(2,1)S(1)}, bf16[4,256,512]{2,1,0:T(8,128)(2,1)S(1)}, u32[]{:S(2)}, u32[]{:S(2)}) collective-permute-start(bf16[4,256,512]{2,1,0:T(8,128)(2,1)S(1)} %get-tuple-element.32), channel_id=1, source_target_pairs={{0,4},{1,5},{2,30},{3,31},{4,8},{5,9},{6,2},{7,3},{8,12},{9,13},{1... | collective-permute-start | bytes 3145736 | tf_op jit(solution)/shard_map/ppermute | solution.py:544
  60.9 21.3 %shard_map.56 = (bf16[4,256,512]{2,1,0:T(8,128)(2,1)S(1)}, bf16[4,256,512]{2,1,0:T(8,128)(2,1)S(1)}, f32[1]{0:T(128)}, bf16[1,256,512]{2,1,0:T(8,128)(2,1)S(1)}) custom-call(f32[6,32]{1,0:T(8,128)S(1)} %select_maximum_fusion.refs_0_, s32[1,2,32]{2,1,0:T(2,128)S(1)} %collective-permute-done.refs_1_, bf16[6,2,256,256]{3,2,1,0:T(8,128)(2,1)S(1)} %select_bitcast_fusion.refs_2_, ...), custom_call_target="tpu_custom_call" | custom-call | flops 53687091200 | bytes 8388608 | tf_op jit(solution)/shard_map/pallas_call | solution.py:416
  82.3 6.1 %collective-permute-start.8 = (bf16[1,256,512]{2,1,0:T(8,128)(2,1)S(1)}, bf16[1,256,512]{2,1,0:T(8,128)(2,1)S(1)}, u32[]{:S(2)}, u32[]{:S(2)}) collective-permute-start(bf16[1,256,512]{2,1,0:T(8,128)(2,1)S(1)} %get-tuple-element.39), channel_id=1, source_target_pairs={{0,2},{1,3},{2,0},{3,1},{4,6},{5,7},{6,4},{7,5},{8,10},{9,11},{10,... | collective-permute-start | bytes 786440 | tf_op jit(solution)/shard_map/ppermute | solution.py:544
  88.3 0.9 copy-done.3
  89.3 18.3 %shard_map.57 = (bf16[3,2,256,256]{3,2,1,0:T(8,128)(2,1)S(1)}, bf16[3,2,256,256]{3,2,1,0:T(8,128)(2,1)S(1)}, f32[1]{0:T(128)}, bf16[1,256,256]{2,1,0:T(8,128)(2,1)S(1)}) custom-call(f32[6,32]{1,0:T(8,128)S(1)} %select_maximum_fusion.refs_0_, s32[1,2,32]{2,1,0:T(2,128)S(1)} %collective-permute-done.refs_1_, ...), custom_call_target="tpu_custom_call" | custom-call | flops 50331648000 | bytes 6291456 | tf_op jit(solution)/shard_map/pallas_call | solution.py:416
  108.3 7.2 %collective-permute-done.7.refs_5_ = bf16[4,256,512]{2,1,0:T(8,128)(2,1)S(1)} collective-permute-done((bf16[4,256,512]{2,1,0:T(8,128)(2,1)S(1)}, bf16[4,256,512]{2,1,0:T(8,128)(2,1)S(1)}, u32[]{:S(2)}, u32[]{:S(2)}) %collective-permute-start.7) | collective-permute-done | bytes 1048608 | tf_op jit(solution)/shard_map/ppermute | solution.py:544
  115.7 21.5 %shard_map.58 = (bf16[5,2,256,256]{3,2,1,0:T(8,128)(2,1)}, bf16[5,2,256,256]{3,2,1,0:T(8,128)(2,1)S(1)}, f32[1]{0:T(128)}) custom-call(f32[6,32]{1,0:T(8,128)S(1)} %select_maximum_fusion.refs_0_, s32[1,2,32]{2,1,0:T(2,128)S(1)} %collective-permute-done.refs_1_, bf16[4,256,512]{2,1,0:T(8,128)(2,1)S(1)} %get-tuple-element.31.refs_2_.refs_3_, ...), custom_call_target="tpu_custom_call" | custom-call | flops 57042534400 | bytes 10485760 | tf_op jit(solution)/shard_map/pallas_call | solution.py:416
  137.3 1.0 collective-permute-done.12.refs_6_
  139.1 4.4 %collective-permute-start.14 = (bf16[5,2,256,256]{3,2,1,0:T(8,128)(2,1)}, bf16[5,2,256,256]{3,2,1,0:T(8,128)(2,1)S(1)}, u32[]{:S(2)}, u32[]{:S(2)}) collective-permute-start(bf16[5,2,256,256]{3,2,1,0:T(8,128)(2,1)} %get-tuple-element.44), channel_id=1, source_target_pairs={{0,30},{1,31},{2,4},{3,5},{4,2},{5,3},{6,8},{7,9},{8,6},{9,7},{10,... | collective-permute-start | bytes 3932168 | tf_op jit(solution)/shard_map/ppermute | solution.py:544
  146.1 2.4 %psum.7.refs_0_ = f32[2]{0:T(128)S(1)} all-reduce(f32[2]{0:T(128)S(1)} %pad_maximum_fusion), channel_id=1, replica_groups=mesh['chain'=16,'block'=2] {'block'}, use_global_device_ids=true, to_apply=%region_0.1 | all-reduce | flops 2 | bytes 16 | tf_op jit(solution)/shard_map/psum | solution.py:635
  148.6 1.3 collective-permute-start.11
  150.6 1.3 collective-permute-start.10
  151.9 6.8 %collective-permute-done.10.refs_1_ = f32[2]{0:T(128)S(1)} collective-permute-done((f32[2]{0:T(128)S(1)}, f32[2]{0:T(128)S(1)}, u32[]{:S(2)}, u32[]{:S(2)}) %collective-permute-start.10) | collective-permute-done | bytes 40 | tf_op jit(solution)/shard_map/ppermute | solution.py:544
  158.7 1.1 copy-done.1
  159.8 2.6 %shard_map.59.refs_4_ = bf16[1,16,2,256,256]{4,3,2,1,0:T(8,128)(2,1)} custom-call(f32[2]{0:T(128)S(1)} %psum.7.refs_0_, f32[2]{0:T(128)S(1)} %collective-permute-done.10.refs_1_, f32[2]{0:T(128)S(1)} %collective-permute-done.11.refs_2_, bf16[5,2,256,256]{3,2,1,0:T(8,128)(2,1)S(1)} %get-tuple-element.45.refs_3_, ...), custom_call_target="tpu_custom_call" | custom-call | bytes 5767168 | tf_op jit(solution)/shard_map/pallas_call | solution.py:518
  162.4 11.9 %collective-permute-done.14.refs_3_ = bf16[5,2,256,256]{3,2,1,0:T(8,128)(2,1)S(1)} collective-permute-done((bf16[5,2,256,256]{3,2,1,0:T(8,128)(2,1)}, bf16[5,2,256,256]{3,2,1,0:T(8,128)(2,1)S(1)}, u32[]{:S(2)}, u32[]{:S(2)}) %collective-permute-start.14) | collective-permute-done | bytes 1310752 | tf_op jit(solution)/shard_map/ppermute | solution.py:544
  174.4 2.1 %shard_map.60 = bf16[1,16,2,256,256]{4,3,2,1,0:T(8,128)(2,1)} custom-call(f32[2]{0:T(128)S(1)} %psum.7.refs_0_, f32[2]{0:T(128)S(1)} %collective-permute-done.10.refs_1_, f32[2]{0:T(128)S(1)} %collective-permute-done.11.refs_2_, bf16[5,2,256,256]{3,2,1,0:T(8,128)(2,1)S(1)} %collective-permute-done.14.refs_3_, ...), custom_call_target="tpu_custom_call", output_to_operand_aliasing={{}: (4, {})} | custom-call | bytes 2621440 | tf_op jit(solution)/shard_map/pallas_call | solution.py:518
  (39 shorter events, 6.3 us)
Async XLA Ops:
  0.0 36.9 %collective-permute-start = (s32[1,2,32]{2,1,0:T(2,128)}, s32[1,2,32]{2,1,0:T(2,128)S(1)}, u32[]{:S(2)}, u32[]{:S(2)}) collective-permute-start(s32[1,2,32]{2,1,0:T(2,128)} %param.7), channel_id=1, source_target_pairs={{0,2},{1,3},{2,0},{3,1},{4,6},{5,7},{6,4},{7,5},{8,10},{9,11},{10,... | collective-permute-start | bytes 776 | tf_op jit(solution)/shard_map/ppermute | solution.py:544
  2.9 3.1 %copy-start.4 = (bf16[1,16,2,256,256]{4,3,2,1,0:T(8,128)(2,1)S(1)}, bf16[1,16,2,256,256]{4,3,2,1,0:T(8,128)(2,1)}, u32[]{:S(2)}) copy-start(bf16[1,16,2,256,256]{4,3,2,1,0:T(8,128)(2,1)} %param.5) | copy-start | bytes 12582916
  6.0 30.6 %collective-permute-start.1 = (bf16[5,2,256,256]{3,2,1,0:T(8,128)(2,1)}, bf16[5,2,256,256]{3,2,1,0:T(8,128)(2,1)}, u32[]{:S(2)}, u32[]{:S(2)}) collective-permute-start(bf16[5,2,256,256]{3,2,1,0:T(8,128)(2,1)} %get-tuple-element.49), channel_id=1, source_target_pairs={{0,2},{1,3},{2,0},{3,1},{4,6},{5,7},{6,4},{7,5},{8,10},{9,11},{10,... | collective-permute-start | bytes 3932168 | tf_op jit(solution)/shard_map/ppermute | solution.py:544
  6.7 30.2 %collective-permute-start.3 = (bf16[1,256,256]{2,1,0:T(8,128)(2,1)}, bf16[1,256,256]{2,1,0:T(8,128)(2,1)S(1)}, u32[]{:S(2)}, u32[]{:S(2)}) collective-permute-start(bf16[1,256,256]{2,1,0:T(8,128)(2,1)} %slice_bitcast_fusion), channel_id=1, source_target_pairs={{2,1},{6,5},{10,9},{14,13},{18,17},{22,21},{26,25},{30,29}} | collective-permute-start | bytes 393224 | tf_op jit(solution)/shard_map/ppermute | solution.py:544
  8.1 28.8 %collective-permute-start.2 = (bf16[1,2,256,256]{3,2,1,0:T(8,128)(2,1)}, bf16[1,2,256,256]{3,2,1,0:T(8,128)(2,1)S(1)}, u32[]{:S(2)}, u32[]{:S(2)}) collective-permute-start(bf16[1,2,256,256]{3,2,1,0:T(8,128)(2,1)} %select_bitcast_fusion.4), channel_id=1, source_target_pairs={{0,1},{3,2},{4,5},{7,6},{8,9},{11,10},{12,13},{15,14},{16,17},{19,... | collective-permute-start | bytes 786440 | tf_op jit(solution)/shard_map/ppermute | solution.py:544
  11.3 0.7 copy-start.6
  11.3 0.7 copy-start.7
  11.3 1.8 %copy-start.5 = (f32[1,2,3]{2,1,0:T(2,128)S(1)}, f32[1,2,3]{2,1,0:T(2,128)}, u32[]{:S(2)}) copy-start(f32[1,2,3]{2,1,0:T(2,128)} %param.9) | copy-start | bytes 76
  13.1 47.9 %copy-start.2 = (bf16[512,256]{0,1:T(8,128)(2,1)}, bf16[512,256]{0,1:T(8,128)(2,1)S(1)}, u32[]{:S(2)}) copy-start(bf16[512,256]{0,1:T(8,128)(2,1)S(1)} %copy.7) | copy-start | bytes 786436
  36.6 24.3 %collective-permute-start.4 = (bf16[4,2,256,256]{3,2,1,0:T(8,128)(2,1)}, bf16[4,2,256,256]{3,2,1,0:T(8,128)(2,1)S(1)}, u32[]{:S(2)}, u32[]{:S(2)}) collective-permute-start(bf16[4,2,256,256]{3,2,1,0:T(8,128)(2,1)} %select_bitcast_fusion.3), channel_id=1, source_target_pairs={{0,2},{1,3},{2,0},{3,1},{4,6},{5,7},{6,4},{7,5},{8,10},{9,11},{10,... | collective-permute-start | bytes 3145736 | tf_op jit(solution)/shard_map/ppermute | solution.py:544
  58.4 29.9 %collective-permute-start.6 = (bf16[1,256,512]{2,1,0:T(8,128)(2,1)S(1)}, bf16[1,256,512]{2,1,0:T(8,128)(2,1)S(1)}, u32[]{:S(2)}, u32[]{:S(2)}) collective-permute-start(bf16[1,256,512]{2,1,0:T(8,128)(2,1)S(1)} %get-tuple-element.33), channel_id=1, source_target_pairs={{1,30},{2,5},{5,2},{6,9},{9,6},{10,13},{13,10},{14,17},{17,14},{18... | collective-permute-start | bytes 786440 | tf_op jit(solution)/shard_map/ppermute | solution.py:544
  59.1 29.2 %collective-permute-start.5 = (bf16[4,256,512]{2,1,0:T(8,128)(2,1)S(1)}, bf16[4,256,512]{2,1,0:T(8,128)(2,1)S(1)}, u32[]{:S(2)}, u32[]{:S(2)}) collective-permute-start(bf16[4,256,512]{2,1,0:T(8,128)(2,1)S(1)} %get-tuple-element.32), channel_id=1, source_target_pairs={{0,4},{1,5},{2,30},{3,31},{4,8},{5,9},{6,2},{7,3},{8,12},{9,13},{1... | collective-permute-start | bytes 3145736 | tf_op jit(solution)/shard_map/ppermute | solution.py:544
  82.3 33.5 %collective-permute-start.8 = (bf16[1,256,512]{2,1,0:T(8,128)(2,1)S(1)}, bf16[1,256,512]{2,1,0:T(8,128)(2,1)S(1)}, u32[]{:S(2)}, u32[]{:S(2)}) collective-permute-start(bf16[1,256,512]{2,1,0:T(8,128)(2,1)S(1)} %get-tuple-element.39), channel_id=1, source_target_pairs={{0,2},{1,3},{2,0},{3,1},{4,6},{5,7},{6,4},{7,5},{8,10},{9,11},{10,... | collective-permute-start | bytes 786440 | tf_op jit(solution)/shard_map/ppermute | solution.py:544
  88.3 27.2 %collective-permute-start.7 = (bf16[4,256,512]{2,1,0:T(8,128)(2,1)S(1)}, bf16[4,256,512]{2,1,0:T(8,128)(2,1)S(1)}, u32[]{:S(2)}, u32[]{:S(2)}) collective-permute-start(bf16[4,256,512]{2,1,0:T(8,128)(2,1)S(1)} %get-tuple-element.37), channel_id=1, source_target_pairs={{0,4},{1,5},{2,30},{3,31},{4,8},{5,9},{6,2},{7,3},{8,12},{9,13},{1... | collective-permute-start | bytes 3145736 | tf_op jit(solution)/shard_map/ppermute | solution.py:544
  88.3 1.0 copy-start.3
  107.6 29.7 %collective-permute-start.13 = (bf16[1,256,256]{2,1,0:T(8,128)(2,1)S(1)}, bf16[1,256,256]{2,1,0:T(8,128)(2,1)S(1)}, u32[]{:S(2)}, u32[]{:S(2)}) collective-permute-start(bf16[1,256,256]{2,1,0:T(8,128)(2,1)S(1)} %get-tuple-element.43), channel_id=1, source_target_pairs={{1,30},{5,2},{9,6},{13,10},{17,14},{21,18},{25,22},{29,26}} | collective-permute-start | bytes 393224 | tf_op jit(solution)/shard_map/ppermute | solution.py:544
  115.5 22.8 %collective-permute-start.12 = (bf16[3,2,256,256]{3,2,1,0:T(8,128)(2,1)S(1)}, bf16[3,2,256,256]{3,2,1,0:T(8,128)(2,1)S(1)}, u32[]{:S(2)}, u32[]{:S(2)}) collective-permute-start(bf16[3,2,256,256]{3,2,1,0:T(8,128)(2,1)S(1)} %get-tuple-element.42), channel_id=1, source_target_pairs={{0,30},{1,31},{2,4},{3,5},{4,2},{5,3},{6,8},{7,9},{8,6},{9,7},{10,... | collective-permute-start | bytes 2359304 | tf_op jit(solution)/shard_map/ppermute | solution.py:544
  138.3 0.9 copy-start
  139.1 35.2 %collective-permute-start.14 = (bf16[5,2,256,256]{3,2,1,0:T(8,128)(2,1)}, bf16[5,2,256,256]{3,2,1,0:T(8,128)(2,1)S(1)}, u32[]{:S(2)}, u32[]{:S(2)}) collective-permute-start(bf16[5,2,256,256]{3,2,1,0:T(8,128)(2,1)} %get-tuple-element.44), channel_id=1, source_target_pairs={{0,30},{1,31},{2,4},{3,5},{4,2},{5,3},{6,8},{7,9},{8,6},{9,7},{10,... | collective-permute-start | bytes 3932168 | tf_op jit(solution)/shard_map/ppermute | solution.py:544
  148.6 3.3 %collective-permute-start.11 = (f32[2]{0:T(128)S(1)}, f32[2]{0:T(128)S(1)}, u32[]{:S(2)}, u32[]{:S(2)}) collective-permute-start(f32[2]{0:T(128)S(1)} %psum.7.refs_0_), channel_id=1, source_target_pairs={{0,4},{1,5},{8,12},{9,13},{16,20},{17,21},{24,28},{25,29}} | collective-permute-start | bytes 32 | tf_op jit(solution)/shard_map/ppermute | solution.py:544
  149.9 0.7 collective-permute-start.9
  150.6 8.2 %collective-permute-start.10 = (f32[2]{0:T(128)S(1)}, f32[2]{0:T(128)S(1)}, u32[]{:S(2)}, u32[]{:S(2)}) collective-permute-start(f32[2]{0:T(128)S(1)} %fusion), channel_id=1, source_target_pairs={{4,8},{5,9},{6,4},{7,5},{12,16},{13,17},{14,12},{15,13},{20,24},{2... | collective-permute-start | bytes 32 | tf_op jit(solution)/shard_map/ppermute | solution.py:544
  158.7 1.1 copy-start.1
